TPU v7x, 32 devices: a whole 2x2x4 slice. The times are simulated.
32 devices in a mesh: grp: 4 (over y, x), in: 8 (over z, core).
Axes of the slice: x: 2, y: 2, z: 4, core: 2. Of those that a mesh axis runs over, the one named last changes fastest.
Arguments:
- unfolding: float32 [1024, 131072], P(None, ('grp', 'in')), may hold values from -300 to 300
- start_basis: float32 [1024, 128], replicated, may hold values from -6 to 6
Outputs:
- factor: float32 [1024, 128], replicated
- core_block: float32 [128, 131072], P(None, ('grp', 'in'))
All inputs are finite; a program needn't handle non-finite values.
Results may differ from a plain program's by a relative error of at most 0.0003.
Values sent between devices are 32-bit elements; how exact they have to be, the bound alone decides.
No kernel may reach another device: no remote copies, remote signals or barrier semaphores. Data moves between devices by JAX's collectives and lax.ppermute only.
A program may use at most 128 MiB of HBM per device.

v0:
```python
import functools

import jax
import jax.numpy as jnp
from jax import lax
from jax.experimental import pallas as pl
from jax.experimental.pallas import tpu as pltpu
from jax.sharding import PartitionSpec as P

ITERS = 3
BLOCKS = 4
F32 = jnp.float32
BF16 = jnp.bfloat16
NT = (((1,), (1,)), ((), ()))
NN = (((1,), (0,)), ((), ()))

CHUNKS = (
    ((0, 1), (0, 2), (1, 2), (0, 3), (1, 3), (2, 3)),
    ((0, 0), (1, 1), (2, 2), (3, 3)),
)


def split(value):
    high = value.astype(BF16)
    low = (value - high.astype(F32)).astype(BF16)
    return high, low


def mm(left, right, dims):
    return lax.dot_general(left, right, dims, preferred_element_type=F32)


def units(chunk, bs):
    for i, j in chunk:
        yield i, j, 0, (bs // 2 if i == j else bs)
        yield i, j, 1, bs


def packed_rows(chunk, bs):
    return sum(rows for *_, rows in units(chunk, bs))


def gram_kernel(bs, steps, u_ref, start_ref, *refs):
    outs = refs[: 2 * len(CHUNKS)]
    start_out, first_ref, second_ref, acc_ref, cross_ref = refs[2 * len(CHUNKS) : 2 * len(CHUNKS) + 5]
    packed_refs = refs[2 * len(CHUNKS) + 5 :]
    buffers = (first_ref, second_ref)
    step = pl.program_id(0)
    depth = u_ref.shape[1]

    def load(ref, part):
        rows = slice(part * bs, (part + 1) * bs)
        high, low = split(u_ref[rows, :])
        ref[rows, 0 * depth : 1 * depth] = high
        ref[rows, 1 * depth : 2 * depth] = high
        ref[rows, 2 * depth : 3 * depth] = low
        ref[rows, 3 * depth : 4 * depth] = high

    def multiply(ref, j):
        above, end = j * bs, (j + 1) * bs
        if j:
            acc_ref[:above, above:end] += mm(
                ref[:above, depth : 4 * depth], ref[above:end, : 3 * depth], NT
            )
        high = ref[above:end, :depth]
        acc_ref[above:end, above:end] += mm(high, high, NT)
        cross_ref[j] += mm(high, ref[above:end, 2 * depth : 3 * depth], NT)

    @pl.when(step == 0)
    def _():
        acc_ref[...] = jnp.zeros_like(acc_ref)
        cross_ref[...] = jnp.zeros_like(cross_ref)
        high, low = split(start_ref[...].T)
        start_out[: high.shape[0], :] = high
        start_out[high.shape[0] :, :] = low
        for part in range(BLOCKS):
            load(buffers[0], part)

    for parity in range(2):

        @pl.when((step > 0) & (step < steps) & (lax.rem(step, 2) == parity))
        def _():
            for j in range(BLOCKS):
                multiply(buffers[1 - parity], BLOCKS - 1 - j)
                load(buffers[parity], j)

    @pl.when(step == steps)
    def _():
        for j in range(BLOCKS):
            multiply(buffers[(steps - 1) % 2], j)
        core = lax.rem(lax.axis_index("in"), 2)
        for j in range(BLOCKS):
            above, end = j * bs, (j + 1) * bs
            acc_ref[above:end, above:end] += cross_ref[j] + cross_ref[j].T
        for number, (chunk, packed) in enumerate(zip(CHUNKS, packed_refs)):
            base = 0
            for i, j, half, height in units(chunk, bs):
                left = j * bs + half * (bs // 2)
                packed[base : base + height, :] = acc_ref[
                    i * bs : i * bs + height, left : left + bs // 2
                ]
                base += height
            sent, kept = outs[2 * number : 2 * number + 2]
            part = sent.shape[0]
            sent[...] = packed[pl.ds(pl.multiple_of((1 - core) * part, part), part), :]
            kept[...] = packed[pl.ds(pl.multiple_of(core * part, part), part), :]


def gram(unfolding, start):
    order, depth = unfolding.shape
    rank = start.shape[1]
    bs = order // BLOCKS
    width = min(512, depth)
    steps = depth // width
    heights = [packed_rows(chunk, bs) for chunk in CHUNKS]
    halves = [(height // 2, bs // 2) for height in heights for _ in range(2)]
    return pl.pallas_call(
        functools.partial(gram_kernel, bs, steps),
        grid=(steps + 1,),
        in_specs=[
            pl.BlockSpec((order, width), lambda k: (0, jnp.minimum(k, steps - 1))),
            pl.BlockSpec((order, rank), lambda k: (0, 0)),
        ],
        out_specs=[pl.BlockSpec(shape, lambda k: (0, 0)) for shape in halves]
        + [pl.BlockSpec((2 * rank, order), lambda k: (0, 0))],
        out_shape=[jax.ShapeDtypeStruct(shape, F32) for shape in halves]
        + [jax.ShapeDtypeStruct((2 * rank, order), BF16)],
        scratch_shapes=[
            pltpu.VMEM((order, 4 * width), BF16),
            pltpu.VMEM((order, 4 * width), BF16),
            pltpu.VMEM((order, order), F32),
            pltpu.VMEM((BLOCKS, bs, bs), F32),
        ]
        + [pltpu.VMEM((height, bs // 2), F32) for height in heights],
        compiler_params=pltpu.CompilerParams(vmem_limit_bytes=60 * 1024 * 1024),
        name="gram",
    )(unfolding, start)


def inverse_cholesky(inner):
    order = inner.shape[0]
    groups = order // 8
    shape = (8, order)
    lane = lax.broadcasted_iota(jnp.int32, shape, 1)
    sub = lax.broadcasted_iota(jnp.int32, shape, 0)

    def lanes(value, k):
        return jnp.broadcast_to(value[:, k : k + 1], shape)

    def subs(value, i):
        return jnp.broadcast_to(value[i : i + 1, :], shape)

    def reciprocal(value):
        guess = pl.reciprocal(value, approx=True)
        return guess * (2.0 - value * guess)

    rows = [inner[8 * m : 8 * m + 8, :] for m in range(groups)]
    result = []
    for b in range(groups):
        first = 8 * b
        inside = (lane >= first) & (lane < first + 8)
        own = rows[b]
        column = [lanes(own, first + k) for k in range(8)]
        s = [[subs(column[k], i) for k in range(i + 1)] for i in range(8)]
        masked = jnp.where(inside, jnp.where(lane == first + sub, 1.0, 0.0), own)
        y = [subs(masked, i) for i in range(8)]
        inverse = [None] * 8
        f = [[None] * 8 for _ in range(8)]
        for k in range(8):
            inverse[k] = reciprocal(s[k][k])
            for i in range(k + 1, 8):
                f[i][k] = s[i][k] * inverse[k]
            for i in range(k + 1, 8):
                for j in range(k + 1, i + 1):
                    s[i][j] = s[i][j] - f[i][k] * s[j][k]
                y[i] = y[i] - f[i][k] * y[k]
        z = [y[k] * inverse[k] for k in range(8)]
        p = list(z)
        for i in range(6, -1, -1):
            for j in range(7, i, -1):
                p[i] = p[i] - f[j][i] * p[j]
        out = y[0] * lax.rsqrt(s[0][0])
        for i in range(1, 8):
            out = jnp.where(sub == i, y[i] * lax.rsqrt(s[i][i]), out)
        result.append(jnp.where(lane <= first + sub, out, 0.0))
        for m in range(b + 1, groups):
            value = jnp.where(inside, 0.0, rows[m])
            if m == b + 1:
                v = [lanes(rows[m], first + k) for k in range(8)]
                for k in range(8):
                    for i in range(k + 1, 8):
                        v[i] = v[i] - f[i][k] * v[k]
                for k in range(8):
                    value = value - v[k] * z[k]
            else:
                for k in range(7, -1, -1):
                    value = value - lanes(rows[m], first + k) * p[k]
            rows[m] = value
    return jnp.concatenate(result, axis=0)


def mm6(left, right, dims):
    return lax.dot_general(
        left, right, dims, precision=lax.Precision.HIGHEST, preferred_element_type=F32
    )


def iterate_kernel(bs, start_ref, *refs):
    count = 2 * len(CHUNKS)
    halves, refs = refs[:count], refs[count:]
    u_hbm, factor_hbm, core_hbm, *refs = refs
    packed_refs, refs = refs[: len(CHUNKS)], refs[len(CHUNKS) :]
    g_high, g_low, both_ref, basis, image, u_vmem, factor_ref, core_ref, sem, out_sem = refs
    rank = basis.shape[0]
    half = bs // 2
    copy = pltpu.make_async_copy(u_hbm, u_vmem, sem)
    copy.start()
    core = lax.rem(lax.axis_index("in"), 2)
    slot = {}
    for number, (chunk, packed) in enumerate(zip(CHUNKS, packed_refs)):
        own, other = halves[2 * number : 2 * number + 2]
        part = own.shape[0]
        packed[pl.ds(pl.multiple_of(core * part, part), part), :] = own[...]
        packed[pl.ds(pl.multiple_of((1 - core) * part, part), part), :] = other[...]
        base = 0
        for i, j, side, height in units(chunk, bs):
            value = packed[base : base + height, :]
            base += height
            place = slot.setdefault((i, j), len(slot))
            high, low = split(value)
            g_high[place, :height, side * half : (side + 1) * half] = high
            g_low[place, :height, side * half : (side + 1) * half] = low
            if i == j and side:
                high, low = split(value[:half].T)
                g_high[place, half:, :half] = high
                g_low[place, half:, :half] = low
    both_ref[...] = start_ref[...]

    def body(_, carry):
        for j in range(BLOCKS):
            total = None
            extra = None
            for i in range(BLOCKS):
                pair, dims = ((i, j), NN) if i <= j else ((j, i), NT)
                cols = slice(i * bs, (i + 1) * bs)
                t = mm(both_ref[:, cols], g_high[slot[pair]], dims)
                e = mm(both_ref[:rank, cols], g_low[slot[pair]], dims)
                total = t if total is None else total + t
                extra = e if extra is None else extra + e
            image[:, j * bs : (j + 1) * bs] = total[:rank] + (total[rank:] + extra)
        inner = mm6(image[...], image[...], NT)
        result = mm6(inverse_cholesky(inner), image[...], NN)
        basis[...] = result
        high, low = split(result)
        both_ref[:rank, :] = high
        both_ref[rank:, :] = low
        return carry

    lax.fori_loop(0, ITERS, body, 0)
    factor_ref[...] = basis[...].T
    depth = u_vmem.shape[1]
    step = min(512, depth)
    outs = [pltpu.make_async_copy(factor_ref, factor_hbm, out_sem.at[0])]
    outs[0].start()
    copy.wait()
    for number, lo in enumerate(range(0, depth, step)):
        cols = slice(lo, lo + step)
        u_high, u_low = split(u_vmem[:, cols])
        total = mm(both_ref[...], u_high, NN)
        core_ref[:, cols] = total[:rank] + (total[rank:] + mm(both_ref[:rank, :], u_low, NN))
        outs.append(
            pltpu.make_async_copy(core_ref.at[:, cols], core_hbm.at[:, cols], out_sem.at[number + 1])
        )
        outs[-1].start()
    for out in outs:
        out.wait()


def iterate(start, halves, unfolding):
    rank = start.shape[0] // 2
    order, depth = unfolding.shape
    bs = order // BLOCKS
    blocks = sum(len(chunk) for chunk in CHUNKS)
    vmem = pl.BlockSpec(memory_space=pltpu.VMEM)
    hbm = pl.BlockSpec(memory_space=pl.ANY)
    return pl.pallas_call(
        functools.partial(iterate_kernel, bs),
        in_specs=[vmem] * (1 + len(halves)) + [hbm],
        out_specs=[hbm, hbm],
        out_shape=[
            jax.ShapeDtypeStruct((order, rank), F32),
            jax.ShapeDtypeStruct((rank, depth), F32),
        ],
        scratch_shapes=[pltpu.VMEM((packed_rows(chunk, bs), bs // 2), F32) for chunk in CHUNKS]
        + [
            pltpu.VMEM((blocks, bs, bs), BF16),
            pltpu.VMEM((blocks, bs, bs), BF16),
            pltpu.VMEM((2 * rank, order), BF16),
            pltpu.VMEM((rank, order), F32),
            pltpu.VMEM((rank, order), F32),
            pltpu.VMEM((order, depth), F32),
            pltpu.VMEM((order, rank), F32),
            pltpu.VMEM((rank, depth), F32),
            pltpu.SemaphoreType.DMA,
            pltpu.SemaphoreType.DMA((1 + depth // min(512, depth),)),
        ],
        compiler_params=pltpu.CompilerParams(vmem_limit_bytes=36 * 1024 * 1024),
        name="iterate",
    )(start, *halves, unfolding)


class Exchange:
    def __init__(self, groups, inner, inner_first):
        self.groups, self.inner = groups, inner
        grp = [("grp", k) for k in range(groups.bit_length() - 1)]
        rest = [("in", k) for k in range(1, inner.bit_length() - 1)]
        flipped = grp[:2][::-1] + grp[2:]
        if inner_first:
            self.orders = tuple(rest[:1] + g + rest[1:] for g in (grp, flipped))
        else:
            self.orders = (grp + rest, flipped + rest)
        self.index = {"grp": lax.axis_index("grp"), "in": lax.axis_index("in")}
        self.core = self.index["in"] & 1

    def swap(self, value, stage):
        pairs = []
        for g in range(self.groups):
            for i in range(self.inner):
                axis, bit = ("in", 0) if stage is None else self.orders[i & 1][stage]
                to = (g ^ (1 << bit), i) if axis == "grp" else (g, i ^ (1 << bit))
                pairs.append((g * self.inner + i, to[0] * self.inner + to[1]))
        return lax.ppermute(value, ("grp", "in"), pairs)

    def bit(self, stage):
        bits = [(self.index[axis] >> k) & 1 for axis, k in (order[stage] for order in self.orders)]
        return jnp.where(self.core == 0, bits[0], bits[1])

    def all_sum(self, sent, kept):
        last = len(self.orders[0]) - 1
        came = self.swap(sent, None)
        for stage in range(last):
            bit = self.bit(stage)
            parts = [x.reshape(2, x.shape[0] // 2, x.shape[1]) for x in (kept, came)]

            def half(place):
                own, new = (lax.dynamic_index_in_dim(x, place, 0, keepdims=False) for x in parts)
                return own + new

            sent, kept = half(1 - bit), half(bit)
            came = self.swap(sent, stage)
        value = kept + came
        value = value + self.swap(value, last)
        for stage in range(last - 1, -1, -1):
            came = self.swap(value, stage)
            bit = self.bit(stage)
            whole = jnp.zeros((2,) + value.shape, value.dtype)
            whole = lax.dynamic_update_index_in_dim(whole, value, bit, 0)
            whole = lax.dynamic_update_index_in_dim(whole, came, 1 - bit, 0)
            value = whole.reshape(-1, value.shape[1])
        return value, self.swap(value, None)


def per_device(groups, inner, unfolding, start_basis):
    *parts, start = gram(unfolding, start_basis)
    halves = []
    for number in range(len(CHUNKS)):
        exchange = Exchange(groups, inner, number > 0)
        halves += exchange.all_sum(*parts[2 * number : 2 * number + 2])
    factor, core_block = iterate(start, halves, unfolding)
    return (factor, core_block)


def solution(mesh):
    in_specs = (P(None, ("grp", "in")), P())
    out_specs = (P(), P(None, ("grp", "in")))
    body = functools.partial(per_device, mesh.shape["grp"], mesh.shape["in"])
    return jax.shard_map(body, mesh=mesh, in_specs=in_specs, out_specs=out_specs, check_vma=False)
```

profile of v0, /device:TPU:0, one launch (start us, length us, event | category | flops | bytes accessed | tf_op | source)
XLA Modules:
  0.0 110.2 jit_solution(11426185333897876298)
XLA Ops:
  0.6 24.4 %gram.1 = (f32[1536,128]{1,0:T(8,128)}, f32[1536,128]{1,0:T(8,128)}, f32[768,128]{1,0:T(8,128)}, f32[768,128]{1,0:T(8,128)}, bf16[256,1024]{1,0:T(8,128)(2,1)}) custom-call(f32[1024,4096]{1,0:T(8,128)} %refs_4_.1, f32[1024,128]{1,0:T(8,128)} %start_ref.1), custom_call_target="tpu_custom_call" | custom-call | tf_op jit(solution)/shard_map/gram/pallas_call | solution.py:117
  25.5 2.1 %collective-permute-done = f32[1536,128]{1,0:T(8,128)S(1)} collective-permute-done((f32[1536,128]{1,0:T(8,128)}, f32[1536,128]{1,0:T(8,128)S(1)}, u32[]{:S(2)}, u32[]{:S(2)}) %collective-permute-start) | collective-permute-done | bytes 786464 | tf_op jit(solution)/shard_map/ppermute | solution.py:332
  27.6 1.2 %dynamic-slice_add_fusion = (f32[1,768,128]{2,1,0:T(8,128)S(1)}, f32[768,128]{1,0:T(8,128)S(1)}) fusion(f32[2,768,128]{2,1,0:T(8,128)S(1)} %bitcast.74, s32[]{:T(128)S(6)} %select_n.74, f32[2,768,128]{2,1,0:T(8,128)} %bitcast.73, s32[]{:T(128)S(6)} %select_n.77), kind=kLoop, calls=%fused_computation.3 | loop fusion | flops 196608 | bytes 2359304 | tf_op jit(solution)/shard_map/add | solution.py:347
  28.8 2.9 %collective-permute-start.1 = (f32[768,128]{1,0:T(8,128)S(1)}, f32[768,128]{1,0:T(8,128)S(1)}, u32[]{:S(2)}, u32[]{:S(2)}) collective-permute-start(f32[768,128]{1,0:T(8,128)S(1)} %get-tuple-element.17), channel_id=1, source_target_pairs={{0,8},{1,17},{2,10},{3,19},{4,12},{5,21},{6,14},{7,23},{8,0},{9,25... | collective-permute-start | bytes 1179656 | tf_op jit(solution)/shard_map/ppermute | solution.py:332
  32.8 1.6 %collective-permute-start.10 = (f32[384,128]{1,0:T(8,128)S(1)}, f32[384,128]{1,0:T(8,128)S(1)}, u32[]{:S(2)}, u32[]{:S(2)}) collective-permute-start(f32[384,128]{1,0:T(8,128)S(1)} %get-tuple-element.19), channel_id=1, source_target_pairs={{0,2},{1,3},{2,0},{3,1},{4,6},{5,7},{6,4},{7,5},{8,10},{9,11},{10,... | collective-permute-start | bytes 589832 | tf_op jit(solution)/shard_map/ppermute | solution.py:332
  34.4 3.0 %collective-permute-done.1 = f32[768,128]{1,0:T(8,128)S(1)} collective-permute-done((f32[768,128]{1,0:T(8,128)S(1)}, f32[768,128]{1,0:T(8,128)S(1)}, u32[]{:S(2)}, u32[]{:S(2)}) %collective-permute-start.1) | collective-permute-done | bytes 393248 | tf_op jit(solution)/shard_map/ppermute | solution.py:332
  37.5 2.1 %collective-permute-start.2 = (f32[384,128]{1,0:T(8,128)S(1)}, f32[384,128]{1,0:T(8,128)S(1)}, u32[]{:S(2)}, u32[]{:S(2)}) collective-permute-start(f32[384,128]{1,0:T(8,128)S(1)} %get-tuple-element.21), channel_id=1, source_target_pairs={{0,16},{1,9},{2,18},{3,11},{4,20},{5,13},{6,22},{7,15},{8,24},{9,1... | collective-permute-start | bytes 589832 | tf_op jit(solution)/shard_map/ppermute | solution.py:332
  39.7 1.6 %collective-permute-start.11 = (f32[192,128]{1,0:T(8,128)S(1)}, f32[192,128]{1,0:T(8,128)S(1)}, u32[]{:S(2)}, u32[]{:S(2)}) collective-permute-start(f32[192,128]{1,0:T(8,128)S(1)} %get-tuple-element.23), channel_id=1, source_target_pairs={{0,8},{1,17},{2,10},{3,19},{4,12},{5,21},{6,14},{7,23},{8,0},{9,25... | collective-permute-start | bytes 294920 | tf_op jit(solution)/shard_map/ppermute | solution.py:332
  41.2 3.1 %collective-permute-done.2 = f32[384,128]{1,0:T(8,128)S(1)} collective-permute-done((f32[384,128]{1,0:T(8,128)S(1)}, f32[384,128]{1,0:T(8,128)S(1)}, u32[]{:S(2)}, u32[]{:S(2)}) %collective-permute-start.2) | collective-permute-done | bytes 196640 | tf_op jit(solution)/shard_map/ppermute | solution.py:332
  44.3 1.8 %collective-permute-start.3 = (f32[192,128]{1,0:T(8,128)S(1)}, f32[192,128]{1,0:T(8,128)S(1)}, u32[]{:S(2)}, u32[]{:S(2)}) collective-permute-start(f32[192,128]{1,0:T(8,128)S(1)} %add_bitcast_fusion.4), channel_id=1, source_target_pairs={{0,2},{1,3},{2,0},{3,1},{4,6},{5,7},{6,4},{7,5},{8,10},{9,11},{10,... | collective-permute-start | bytes 294920 | tf_op jit(solution)/shard_map/ppermute | solution.py:332
  46.1 1.6 %collective-permute-start.12 = (f32[96,128]{1,0:T(8,128)S(1)}, f32[96,128]{1,0:T(8,128)S(1)}, u32[]{:S(2)}, u32[]{:S(2)}) collective-permute-start(f32[96,128]{1,0:T(8,128)S(1)} %add_bitcast_fusion.5), channel_id=1, source_target_pairs={{0,16},{1,9},{2,18},{3,11},{4,20},{5,13},{6,22},{7,15},{8,24},{9,1... | collective-permute-start | bytes 147464 | tf_op jit(solution)/shard_map/ppermute | solution.py:332
  47.7 1.3 %collective-permute-done.3 = f32[192,128]{1,0:T(8,128)S(1)} collective-permute-done((f32[192,128]{1,0:T(8,128)S(1)}, f32[192,128]{1,0:T(8,128)S(1)}, u32[]{:S(2)}, u32[]{:S(2)}) %collective-permute-start.3) | collective-permute-done | bytes 98336 | tf_op jit(solution)/shard_map/ppermute | solution.py:332
  49.0 3.6 %collective-permute-start.4 = (f32[192,128]{1,0:T(8,128)S(1)}, f32[192,128]{1,0:T(8,128)S(1)}, u32[]{:S(2)}, u32[]{:S(2)}) collective-permute-start(f32[192,128]{1,0:T(8,128)S(1)} %bitcast_add_fusion), channel_id=1, source_target_pairs={{0,4},{1,5},{2,6},{3,7},{4,0},{5,1},{6,2},{7,3},{8,12},{9,13},{10,... | collective-permute-start | bytes 294920 | tf_op jit(solution)/shard_map/ppermute | solution.py:332
  53.0 3.3 %collective-permute-done.4 = f32[192,128]{1,0:T(8,128)S(1)} collective-permute-done((f32[192,128]{1,0:T(8,128)S(1)}, f32[192,128]{1,0:T(8,128)S(1)}, u32[]{:S(2)}, u32[]{:S(2)}) %collective-permute-start.4) | collective-permute-done | bytes 98336 | tf_op jit(solution)/shard_map/ppermute | solution.py:332
  56.5 1.7 %collective-permute-done.13 = f32[96,128]{1,0:T(8,128)S(1)} collective-permute-done((f32[96,128]{1,0:T(8,128)S(1)}, f32[96,128]{1,0:T(8,128)S(1)}, u32[]{:S(2)}, u32[]{:S(2)}) %collective-permute-start.13) | collective-permute-done | bytes 49184 | tf_op jit(solution)/shard_map/ppermute | solution.py:332
  58.3 1.6 %collective-permute-start.14 = (f32[96,128]{1,0:T(8,128)S(1)}, f32[96,128]{1,0:T(8,128)S(1)}, u32[]{:S(2)}, u32[]{:S(2)}) collective-permute-start(f32[96,128]{1,0:T(8,128)S(1)} %get-tuple-element.13), channel_id=1, source_target_pairs={{0,16},{1,9},{2,18},{3,11},{4,20},{5,13},{6,22},{7,15},{8,24},{9,1... | collective-permute-start | bytes 147464 | tf_op jit(solution)/shard_map/ppermute | solution.py:332
  59.9 1.2 %collective-permute-done.5 = f32[192,128]{1,0:T(8,128)S(1)} collective-permute-done((f32[192,128]{1,0:T(8,128)S(1)}, f32[192,128]{1,0:T(8,128)S(1)}, u32[]{:S(2)}, u32[]{:S(2)}) %collective-permute-start.5) | collective-permute-done | bytes 98336 | tf_op jit(solution)/shard_map/ppermute | solution.py:332
  61.0 1.6 %collective-permute-start.6 = (f32[384,128]{1,0:T(8,128)S(1)}, f32[384,128]{1,0:T(8,128)S(1)}, u32[]{:S(2)}, u32[]{:S(2)}) collective-permute-start(f32[384,128]{1,0:T(8,128)S(1)} %bitcast.69), channel_id=1, source_target_pairs={{0,16},{1,9},{2,18},{3,11},{4,20},{5,13},{6,22},{7,15},{8,24},{9,1... | collective-permute-start | bytes 589832 | tf_op jit(solution)/shard_map/ppermute | solution.py:332
  62.6 1.8 %collective-permute-start.15 = (f32[192,128]{1,0:T(8,128)S(1)}, f32[192,128]{1,0:T(8,128)S(1)}, u32[]{:S(2)}, u32[]{:S(2)}) collective-permute-start(f32[192,128]{1,0:T(8,128)S(1)} %bitcast.80), channel_id=1, source_target_pairs={{0,8},{1,17},{2,10},{3,19},{4,12},{5,21},{6,14},{7,23},{8,0},{9,25... | collective-permute-start | bytes 294920 | tf_op jit(solution)/shard_map/ppermute | solution.py:332
  64.4 4.5 %collective-permute-done.6 = f32[384,128]{1,0:T(8,128)S(1)} collective-permute-done((f32[384,128]{1,0:T(8,128)S(1)}, f32[384,128]{1,0:T(8,128)S(1)}, u32[]{:S(2)}, u32[]{:S(2)}) %collective-permute-start.6) | collective-permute-done | bytes 196640 | tf_op jit(solution)/shard_map/ppermute | solution.py:332
  69.0 1.9 %collective-permute-start.7 = (f32[768,128]{1,0:T(8,128)S(1)}, f32[768,128]{1,0:T(8,128)S(1)}, u32[]{:S(2)}, u32[]{:S(2)}) collective-permute-start(f32[768,128]{1,0:T(8,128)S(1)} %bitcast.66), channel_id=1, source_target_pairs={{0,8},{1,17},{2,10},{3,19},{4,12},{5,21},{6,14},{7,23},{8,0},{9,25... | collective-permute-start | bytes 1179656 | tf_op jit(solution)/shard_map/ppermute | solution.py:332
  72.1 4.7 %collective-permute-done.7 = f32[768,128]{1,0:T(8,128)S(1)} collective-permute-done((f32[768,128]{1,0:T(8,128)S(1)}, f32[768,128]{1,0:T(8,128)S(1)}, u32[]{:S(2)}, u32[]{:S(2)}) %collective-permute-start.7) | collective-permute-done | bytes 393248 | tf_op jit(solution)/shard_map/ppermute | solution.py:332
  77.6 2.2 %collective-permute-done.17.refs_3_ = f32[768,128]{1,0:T(8,128)S(1)} collective-permute-done((f32[768,128]{1,0:T(8,128)S(1)}, f32[768,128]{1,0:T(8,128)S(1)}, u32[]{:S(2)}, u32[]{:S(2)}) %collective-permute-start.17) | collective-permute-done | bytes 393248 | tf_op jit(solution)/shard_map/ppermute | solution.py:332
  80.8 29.3 %iterate.1 = (f32[1024,128]{1,0:T(8,128)}, f32[128,4096]{1,0:T(8,128)}) custom-call(bf16[256,1024]{1,0:T(8,128)(2,1)S(1)} %copy-done, f32[1536,128]{1,0:T(8,128)S(1)} %bitcast.63, f32[1536,128]{1,0:T(8,128)S(1)} %collective-permute-done.8.refs_1_, f32[768,128]{1,0:T(8,128)S(1)} %bitcast.65, f32[768,128]{1,0:T(8,128)S(1)} %collective-permute-done.17.refs_3_, ...), custom_call_target="tpu_custom_call" | custom-call | tf_op jit(solution)/shard_map/iterate/pallas_call | solution.py:286
  (42 shorter events, 5.3 us)
Async XLA Ops:
  25.0 2.6 %collective-permute-start = (f32[1536,128]{1,0:T(8,128)}, f32[1536,128]{1,0:T(8,128)S(1)}, u32[]{:S(2)}, u32[]{:S(2)}) collective-permute-start(f32[1536,128]{1,0:T(8,128)} %get-tuple-element.9), channel_id=1, source_target_pairs={{0,1},{1,0},{2,3},{3,2},{4,5},{5,4},{6,7},{7,6},{8,9},{9,8},{10,11... | collective-permute-start | bytes 2359304 | tf_op jit(solution)/shard_map/ppermute | solution.py:332
  25.5 6.2 %collective-permute-start.9 = (f32[768,128]{1,0:T(8,128)}, f32[768,128]{1,0:T(8,128)S(1)}, u32[]{:S(2)}, u32[]{:S(2)}) collective-permute-start(f32[768,128]{1,0:T(8,128)} %get-tuple-element.11), channel_id=1, source_target_pairs={{0,1},{1,0},{2,3},{3,2},{4,5},{5,4},{6,7},{7,6},{8,9},{9,8},{10,11... | collective-permute-start | bytes 1179656 | tf_op jit(solution)/shard_map/ppermute | solution.py:332
  28.8 8.7 %collective-permute-start.1 = (f32[768,128]{1,0:T(8,128)S(1)}, f32[768,128]{1,0:T(8,128)S(1)}, u32[]{:S(2)}, u32[]{:S(2)}) collective-permute-start(f32[768,128]{1,0:T(8,128)S(1)} %get-tuple-element.17), channel_id=1, source_target_pairs={{0,8},{1,17},{2,10},{3,19},{4,12},{5,21},{6,14},{7,23},{8,0},{9,25... | collective-permute-start | bytes 1179656 | tf_op jit(solution)/shard_map/ppermute | solution.py:332
  32.8 6.8 %collective-permute-start.10 = (f32[384,128]{1,0:T(8,128)S(1)}, f32[384,128]{1,0:T(8,128)S(1)}, u32[]{:S(2)}, u32[]{:S(2)}) collective-permute-start(f32[384,128]{1,0:T(8,128)S(1)} %get-tuple-element.19), channel_id=1, source_target_pairs={{0,2},{1,3},{2,0},{3,1},{4,6},{5,7},{6,4},{7,5},{8,10},{9,11},{10,... | collective-permute-start | bytes 589832 | tf_op jit(solution)/shard_map/ppermute | solution.py:332
  37.5 6.8 %collective-permute-start.2 = (f32[384,128]{1,0:T(8,128)S(1)}, f32[384,128]{1,0:T(8,128)S(1)}, u32[]{:S(2)}, u32[]{:S(2)}) collective-permute-start(f32[384,128]{1,0:T(8,128)S(1)} %get-tuple-element.21), channel_id=1, source_target_pairs={{0,16},{1,9},{2,18},{3,11},{4,20},{5,13},{6,22},{7,15},{8,24},{9,1... | collective-permute-start | bytes 589832 | tf_op jit(solution)/shard_map/ppermute | solution.py:332
  39.7 6.5 %collective-permute-start.11 = (f32[192,128]{1,0:T(8,128)S(1)}, f32[192,128]{1,0:T(8,128)S(1)}, u32[]{:S(2)}, u32[]{:S(2)}) collective-permute-start(f32[192,128]{1,0:T(8,128)S(1)} %get-tuple-element.23), channel_id=1, source_target_pairs={{0,8},{1,17},{2,10},{3,19},{4,12},{5,21},{6,14},{7,23},{8,0},{9,25... | collective-permute-start | bytes 294920 | tf_op jit(solution)/shard_map/ppermute | solution.py:332
  44.3 4.7 %collective-permute-start.3 = (f32[192,128]{1,0:T(8,128)S(1)}, f32[192,128]{1,0:T(8,128)S(1)}, u32[]{:S(2)}, u32[]{:S(2)}) collective-permute-start(f32[192,128]{1,0:T(8,128)S(1)} %add_bitcast_fusion.4), channel_id=1, source_target_pairs={{0,2},{1,3},{2,0},{3,1},{4,6},{5,7},{6,4},{7,5},{8,10},{9,11},{10,... | collective-permute-start | bytes 294920 | tf_op jit(solution)/shard_map/ppermute | solution.py:332
  46.1 6.5 %collective-permute-start.12 = (f32[96,128]{1,0:T(8,128)S(1)}, f32[96,128]{1,0:T(8,128)S(1)}, u32[]{:S(2)}, u32[]{:S(2)}) collective-permute-start(f32[96,128]{1,0:T(8,128)S(1)} %add_bitcast_fusion.5), channel_id=1, source_target_pairs={{0,16},{1,9},{2,18},{3,11},{4,20},{5,13},{6,22},{7,15},{8,24},{9,1... | collective-permute-start | bytes 147464 | tf_op jit(solution)/shard_map/ppermute | solution.py:332
  49.0 7.3 %collective-permute-start.4 = (f32[192,128]{1,0:T(8,128)S(1)}, f32[192,128]{1,0:T(8,128)S(1)}, u32[]{:S(2)}, u32[]{:S(2)}) collective-permute-start(f32[192,128]{1,0:T(8,128)S(1)} %bitcast_add_fusion), channel_id=1, source_target_pairs={{0,4},{1,5},{2,6},{3,7},{4,0},{5,1},{6,2},{7,3},{8,12},{9,13},{10,... | collective-permute-start | bytes 294920 | tf_op jit(solution)/shard_map/ppermute | solution.py:332
  52.7 5.6 %collective-permute-start.13 = (f32[96,128]{1,0:T(8,128)S(1)}, f32[96,128]{1,0:T(8,128)S(1)}, u32[]{:S(2)}, u32[]{:S(2)}) collective-permute-start(f32[96,128]{1,0:T(8,128)S(1)} %bitcast_add_fusion.1), channel_id=1, source_target_pairs={{0,4},{1,5},{2,6},{3,7},{4,0},{5,1},{6,2},{7,3},{8,12},{9,13},{10,... | collective-permute-start | bytes 147464 | tf_op jit(solution)/shard_map/ppermute | solution.py:332
  56.3 4.7 %collective-permute-start.5 = (f32[192,128]{1,0:T(8,128)S(1)}, f32[192,128]{1,0:T(8,128)S(1)}, u32[]{:S(2)}, u32[]{:S(2)}) collective-permute-start(f32[192,128]{1,0:T(8,128)S(1)} %get-tuple-element.15), channel_id=1, source_target_pairs={{0,2},{1,3},{2,0},{3,1},{4,6},{5,7},{6,4},{7,5},{8,10},{9,11},{10,... | collective-permute-start | bytes 294920 | tf_op jit(solution)/shard_map/ppermute | solution.py:332
  58.3 4.3 %collective-permute-start.14 = (f32[96,128]{1,0:T(8,128)S(1)}, f32[96,128]{1,0:T(8,128)S(1)}, u32[]{:S(2)}, u32[]{:S(2)}) collective-permute-start(f32[96,128]{1,0:T(8,128)S(1)} %get-tuple-element.13), channel_id=1, source_target_pairs={{0,16},{1,9},{2,18},{3,11},{4,20},{5,13},{6,22},{7,15},{8,24},{9,1... | collective-permute-start | bytes 147464 | tf_op jit(solution)/shard_map/ppermute | solution.py:332
  61.0 7.9 %collective-permute-start.6 = (f32[384,128]{1,0:T(8,128)S(1)}, f32[384,128]{1,0:T(8,128)S(1)}, u32[]{:S(2)}, u32[]{:S(2)}) collective-permute-start(f32[384,128]{1,0:T(8,128)S(1)} %bitcast.69), channel_id=1, source_target_pairs={{0,16},{1,9},{2,18},{3,11},{4,20},{5,13},{6,22},{7,15},{8,24},{9,1... | collective-permute-start | bytes 589832 | tf_op jit(solution)/shard_map/ppermute | solution.py:332
  62.6 8.3 %collective-permute-start.15 = (f32[192,128]{1,0:T(8,128)S(1)}, f32[192,128]{1,0:T(8,128)S(1)}, u32[]{:S(2)}, u32[]{:S(2)}) collective-permute-start(f32[192,128]{1,0:T(8,128)S(1)} %bitcast.80), channel_id=1, source_target_pairs={{0,8},{1,17},{2,10},{3,19},{4,12},{5,21},{6,14},{7,23},{8,0},{9,25... | collective-permute-start | bytes 294920 | tf_op jit(solution)/shard_map/ppermute | solution.py:332
  69.0 7.8 %collective-permute-start.7 = (f32[768,128]{1,0:T(8,128)S(1)}, f32[768,128]{1,0:T(8,128)S(1)}, u32[]{:S(2)}, u32[]{:S(2)}) collective-permute-start(f32[768,128]{1,0:T(8,128)S(1)} %bitcast.66), channel_id=1, source_target_pairs={{0,8},{1,17},{2,10},{3,19},{4,12},{5,21},{6,14},{7,23},{8,0},{9,25... | collective-permute-start | bytes 1179656 | tf_op jit(solution)/shard_map/ppermute | solution.py:332
  71.0 6.0 %collective-permute-start.16 = (f32[384,128]{1,0:T(8,128)S(1)}, f32[384,128]{1,0:T(8,128)S(1)}, u32[]{:S(2)}, u32[]{:S(2)}) collective-permute-start(f32[384,128]{1,0:T(8,128)S(1)} %bitcast.71), channel_id=1, source_target_pairs={{0,2},{1,3},{2,0},{3,1},{4,6},{5,7},{6,4},{7,5},{8,10},{9,11},{10,... | collective-permute-start | bytes 589832 | tf_op jit(solution)/shard_map/ppermute | solution.py:332
  76.8 2.9 %collective-permute-start.8 = (f32[1536,128]{1,0:T(8,128)S(1)}, f32[1536,128]{1,0:T(8,128)S(1)}, u32[]{:S(2)}, u32[]{:S(2)}) collective-permute-start(f32[1536,128]{1,0:T(8,128)S(1)} %bitcast.62), channel_id=1, source_target_pairs={{0,1},{1,0},{2,3},{3,2},{4,5},{5,4},{6,7},{7,6},{8,9},{9,8},{10,11... | collective-permute-start | bytes 2359304 | tf_op jit(solution)/shard_map/ppermute | solution.py:332
  77.0 2.7 %collective-permute-start.17 = (f32[768,128]{1,0:T(8,128)S(1)}, f32[768,128]{1,0:T(8,128)S(1)}, u32[]{:S(2)}, u32[]{:S(2)}) collective-permute-start(f32[768,128]{1,0:T(8,128)S(1)} %bitcast.64), channel_id=1, source_target_pairs={{0,1},{1,0},{2,3},{3,2},{4,5},{5,4},{6,7},{7,6},{8,9},{9,8},{10,11... | collective-permute-start | bytes 1179656 | tf_op jit(solution)/shard_map/ppermute | solution.py:332
  79.8 1.0 copy-start
where the time goes:
time: 110 us
  Pallas kernels  53.6 us (49%)
  waiting for transfers between devices  27.2 us (25%)
  starting transfers between devices  24.7 us (22%)
  other arithmetic  2.4 us (2%)
  local copies, waits for them, and re-layouts  1.37 us (1%)
    pallas_call x1, Pallas kernels, iterate(): pl.pallas_call(functools.partial(iterate_kernel, bs), in_specs=[vmem] * (...  29.3 us
    ppermute x18, waiting for transfers between devices, swap(): return lax.ppermute(value, ('grp', 'in'), pairs)  27.2 us
    ppermute x18, starting transfers between devices, swap(): return lax.ppermute(value, ('grp', 'in'), pairs)  24.7 us
    pallas_call x1, Pallas kernels, gram(): pl.pallas_call(functools.partial(gram_kernel, bs, steps), grid=(steps + 1...  24.4 us
    add x6, other arithmetic, half(): return own + new  2.34 us
  transfers between devices with their start and end apart: 18, of which 10 were waited for; matrix products, arithmetic and copies ran while one was open for 2% of the time, Pallas kernels for 0%

commit v1 on v0

v1 whole, which is shorter than its diff:
```python
import functools

import jax
import jax.numpy as jnp
from jax import lax
from jax.experimental import pallas as pl
from jax.experimental.pallas import tpu as pltpu
from jax.sharding import PartitionSpec as P

ITERS = 3
BLOCKS = 4
F32 = jnp.float32
BF16 = jnp.bfloat16
NT = (((1,), (1,)), ((), ()))
NN = (((1,), (0,)), ((), ()))

CHUNKS = (
    ((0, 3), (1, 3), (2, 3), (3, 3), (0, 0)),
    ((0, 2), (1, 2), (2, 2), (0, 1), (1, 1)),
)


def split(value):
    high = value.astype(BF16)
    low = (value - high.astype(F32)).astype(BF16)
    return high, low


def mm(left, right, dims):
    return lax.dot_general(left, right, dims, preferred_element_type=F32)


def units(chunk, bs):
    for i, j in chunk:
        yield i, j, 0, (bs // 2 if i == j else bs)
        yield i, j, 1, bs


def packed_rows(chunk, bs):
    return sum(rows for *_, rows in units(chunk, bs))


def gram_kernel(bs, widths, u_hbm, *refs):
    count = len(CHUNKS)
    outs, packed_refs = refs[: 2 * count], refs[2 * count : 3 * count]
    u_ref, parts_ref, acc_ref, cross_ref, sems = refs[3 * count :]
    copies = []
    first = 0
    for number, width in enumerate(widths):
        cols = slice(first, first + width)
        copies.append(pltpu.make_async_copy(u_hbm.at[:, cols], u_ref.at[:, cols], sems.at[number]))
        copies[-1].start()
        first += width

    def add(ref, place, value, new):
        ref[place] = value if new else ref[place] + value

    first = 0
    for number, width in enumerate(widths):
        copies[number].wait()
        for j in range(BLOCKS):
            rows = slice(j * bs, (j + 1) * bs)
            high, low = split(u_ref[rows, first : first + width])
            for place, value in enumerate((high, high, low, high)):
                parts_ref[rows, place * width : (place + 1) * width] = value
        first += width
        for j in range(BLOCKS):
            above, end = j * bs, (j + 1) * bs
            if j:
                value = mm(
                    parts_ref[:above, width : 4 * width], parts_ref[above:end, : 3 * width], NT
                )
                add(acc_ref, (slice(0, above), slice(above, end)), value, number == 0)
            high = parts_ref[above:end, :width]
            low = parts_ref[above:end, 2 * width : 3 * width]
            own = (slice(above, end), slice(above, end))
            add(acc_ref, own, mm(high, high, NT), number == 0)
            add(cross_ref, j, mm(high, low, NT), number == 0)

    core = lax.rem(lax.axis_index("in"), 2)
    for j in range(BLOCKS):
        above, end = j * bs, (j + 1) * bs
        acc_ref[above:end, above:end] += cross_ref[j] + cross_ref[j].T
    for number, (chunk, packed) in enumerate(zip(CHUNKS, packed_refs)):
        base = 0
        for i, j, half, height in units(chunk, bs):
            left = j * bs + half * (bs // 2)
            packed[base : base + height, :] = acc_ref[
                i * bs : i * bs + height, left : left + bs // 2
            ]
            base += height
        sent, kept = outs[2 * number : 2 * number + 2]
        part = sent.shape[0]
        sent[...] = packed[pl.ds(pl.multiple_of((1 - core) * part, part), part), :]
        kept[...] = packed[pl.ds(pl.multiple_of(core * part, part), part), :]


def gram(unfolding):
    order, depth = unfolding.shape
    bs = order // BLOCKS
    widths = (depth // 8, 3 * depth // 8, depth // 2)
    heights = [packed_rows(chunk, bs) for chunk in CHUNKS]
    halves = [(height // 2, bs // 2) for height in heights for _ in range(2)]
    return pl.pallas_call(
        functools.partial(gram_kernel, bs, widths),
        in_specs=[pl.BlockSpec(memory_space=pl.ANY)],
        out_specs=[pl.BlockSpec(memory_space=pltpu.VMEM)] * len(halves),
        out_shape=[pltpu.VMEM(shape, F32) for shape in halves],
        scratch_shapes=[pltpu.VMEM((height, bs // 2), F32) for height in heights]
        + [
            pltpu.VMEM((order, depth), F32),
            pltpu.VMEM((order, 4 * max(widths)), BF16),
            pltpu.VMEM((order, order), F32),
            pltpu.VMEM((BLOCKS, bs, bs), F32),
            pltpu.SemaphoreType.DMA((len(widths),)),
        ],
        compiler_params=pltpu.CompilerParams(vmem_limit_bytes=50 * 1024 * 1024),
        name="gram",
    )(unfolding)


def inverse_cholesky(inner):
    order = inner.shape[0]
    size = min(16, order)
    shape = (8, order)
    lane = lax.broadcasted_iota(jnp.int32, shape, 1)
    sub = lax.broadcasted_iota(jnp.int32, shape, 0)

    def lanes(value, k):
        return jnp.broadcast_to(value[:, k : k + 1], shape)

    def subs(value, i):
        return jnp.broadcast_to(value[i : i + 1, :], shape)

    def reciprocal(value):
        guess = pl.reciprocal(value, approx=True)
        return guess * (2.0 - value * guess)

    rows = [inner[m : m + 8, :] for m in range(0, order, 8)]
    result = []
    for first in range(0, order, size):
        inside = (lane >= first) & (lane < first + size)
        own = rows[first // 8 : (first + size) // 8]
        s = [[None] * (i + 1) for i in range(size)]
        for k in range(size):
            for g in range(k // 8, size // 8):
                column = lanes(own[g], first + k)
                for i in range(max(k, 8 * g), 8 * g + 8):
                    s[i][k] = subs(column, i - 8 * g)
        y = []
        for g in range(size // 8):
            unit = jnp.where(lane == first + 8 * g + sub, 1.0, 0.0)
            masked = jnp.where(inside, unit, own[g])
            y += [subs(masked, i) for i in range(8)]
        inverse = [None] * size
        f = [[None] * size for _ in range(size)]
        for k in range(size):
            inverse[k] = reciprocal(s[k][k])
            for i in range(k + 1, size):
                f[i][k] = s[i][k] * inverse[k]
            for i in range(k + 1, size):
                for j in range(k + 1, i + 1):
                    s[i][j] = s[i][j] - f[i][k] * s[j][k]
                y[i] = y[i] - f[i][k] * y[k]
        p = [y[k] * inverse[k] for k in range(size)]
        for j in range(size - 1, 0, -1):
            for i in range(j - 1, -1, -1):
                p[i] = p[i] - f[j][i] * p[j]
        for g in range(size // 8):
            out = y[8 * g] * lax.rsqrt(s[8 * g][8 * g])
            for i in range(1, 8):
                out = jnp.where(sub == i, y[8 * g + i] * lax.rsqrt(s[8 * g + i][8 * g + i]), out)
            result.append(jnp.where(lane <= first + 8 * g + sub, out, 0.0))
        for m in range((first + size) // 8, order // 8):
            value = jnp.where(inside, 0.0, rows[m])
            for k in range(size - 1, -1, -1):
                value = value - lanes(rows[m], first + k) * p[k]
            rows[m] = value
    return jnp.concatenate(result, axis=0)


def mm6(left, right, dims):
    return lax.dot_general(
        left, right, dims, precision=lax.Precision.HIGHEST, preferred_element_type=F32
    )


def iterate_kernel(bs, start_hbm, *refs):
    count = 2 * len(CHUNKS)
    halves, refs = refs[:count], refs[count:]
    u_hbm, factor_hbm, core_hbm, *refs = refs
    packed_refs, refs = refs[: len(CHUNKS)], refs[len(CHUNKS) :]
    g_high, g_low, both_ref, basis, image, u_vmem, factor_ref, core_ref, sems, out_sem = refs
    rank = basis.shape[0]
    half = bs // 2
    start_copy = pltpu.make_async_copy(start_hbm, factor_ref, sems.at[0])
    start_copy.start()
    copy = pltpu.make_async_copy(u_hbm, u_vmem, sems.at[1])
    copy.start()
    core = lax.rem(lax.axis_index("in"), 2)
    slot = {}
    for number, (chunk, packed) in enumerate(zip(CHUNKS, packed_refs)):
        own, other = halves[2 * number : 2 * number + 2]
        part = own.shape[0]
        packed[pl.ds(pl.multiple_of(core * part, part), part), :] = own[...]
        packed[pl.ds(pl.multiple_of((1 - core) * part, part), part), :] = other[...]
        base = 0
        for i, j, side, height in units(chunk, bs):
            value = packed[base : base + height, :]
            base += height
            place = slot.setdefault((i, j), len(slot))
            high, low = split(value)
            g_high[place, :height, side * half : (side + 1) * half] = high
            g_low[place, :height, side * half : (side + 1) * half] = low
            if i == j and side:
                high, low = split(value[:half].T)
                g_high[place, half:, :half] = high
                g_low[place, half:, :half] = low
    start_copy.wait()
    high, low = split(factor_ref[...].T)
    both_ref[:rank, :] = high
    both_ref[rank:, :] = low

    def body(_, carry):
        for j in range(BLOCKS):
            total = None
            extra = None
            for i in range(BLOCKS):
                pair, dims = ((i, j), NN) if i <= j else ((j, i), NT)
                cols = slice(i * bs, (i + 1) * bs)
                t = mm(both_ref[:, cols], g_high[slot[pair]], dims)
                e = mm(both_ref[:rank, cols], g_low[slot[pair]], dims)
                total = t if total is None else total + t
                extra = e if extra is None else extra + e
            image[:, j * bs : (j + 1) * bs] = total[:rank] + (total[rank:] + extra)
        inner = mm6(image[...], image[...], NT)
        result = mm6(inverse_cholesky(inner), image[...], NN)
        basis[...] = result
        high, low = split(result)
        both_ref[:rank, :] = high
        both_ref[rank:, :] = low
        return carry

    lax.fori_loop(0, ITERS, body, 0)
    factor_ref[...] = basis[...].T
    depth = u_vmem.shape[1]
    step = min(512, depth)
    outs = [pltpu.make_async_copy(factor_ref, factor_hbm, out_sem.at[0])]
    outs[0].start()
    copy.wait()
    for number, lo in enumerate(range(0, depth, step)):
        cols = slice(lo, lo + step)
        u_high, u_low = split(u_vmem[:, cols])
        total = mm(both_ref[...], u_high, NN)
        core_ref[:, cols] = total[:rank] + (total[rank:] + mm(both_ref[:rank, :], u_low, NN))
        outs.append(
            pltpu.make_async_copy(core_ref.at[:, cols], core_hbm.at[:, cols], out_sem.at[number + 1])
        )
        outs[-1].start()
    for out in outs:
        out.wait()


def iterate(start, halves, unfolding):
    order, rank = start.shape
    depth = unfolding.shape[1]
    bs = order // BLOCKS
    blocks = sum(len(chunk) for chunk in CHUNKS)
    vmem = pl.BlockSpec(memory_space=pltpu.VMEM)
    hbm = pl.BlockSpec(memory_space=pl.ANY)
    return pl.pallas_call(
        functools.partial(iterate_kernel, bs),
        in_specs=[hbm] + [vmem] * len(halves) + [hbm],
        out_specs=[hbm, hbm],
        out_shape=[
            jax.ShapeDtypeStruct((order, rank), F32),
            jax.ShapeDtypeStruct((rank, depth), F32),
        ],
        scratch_shapes=[pltpu.VMEM((packed_rows(chunk, bs), bs // 2), F32) for chunk in CHUNKS]
        + [
            pltpu.VMEM((blocks, bs, bs), BF16),
            pltpu.VMEM((blocks, bs, bs), BF16),
            pltpu.VMEM((2 * rank, order), BF16),
            pltpu.VMEM((rank, order), F32),
            pltpu.VMEM((rank, order), F32),
            pltpu.VMEM((order, depth), F32),
            pltpu.VMEM((order, rank), F32),
            pltpu.VMEM((rank, depth), F32),
            pltpu.SemaphoreType.DMA((2,)),
            pltpu.SemaphoreType.DMA((1 + depth // min(512, depth),)),
        ],
        compiler_params=pltpu.CompilerParams(vmem_limit_bytes=36 * 1024 * 1024),
        name="iterate",
    )(start, *halves, unfolding)


class Exchange:
    def __init__(self, groups, inner):
        self.groups, self.inner = groups, inner
        grp = [("grp", k) for k in range(groups.bit_length() - 1)]
        rest = [("in", k) for k in range(1, inner.bit_length() - 1)]
        self.orders = (grp + rest, grp[:2][::-1] + grp[2:] + rest)
        self.index = {"grp": lax.axis_index("grp"), "in": lax.axis_index("in")}
        self.core = self.index["in"] & 1

    def swap(self, value, stage):
        pairs = []
        for g in range(self.groups):
            for i in range(self.inner):
                axis, bit = ("in", 0) if stage is None else self.orders[i & 1][stage]
                to = (g ^ (1 << bit), i) if axis == "grp" else (g, i ^ (1 << bit))
                pairs.append((g * self.inner + i, to[0] * self.inner + to[1]))
        return lax.ppermute(value, ("grp", "in"), pairs)

    def bit(self, stage):
        bits = [(self.index[axis] >> k) & 1 for axis, k in (order[stage] for order in self.orders)]
        return jnp.where(self.core == 0, bits[0], bits[1])

    def all_sum(self, sent, kept):
        last = len(self.orders[0]) - 1
        came = self.swap(sent, None)
        for stage in range(last):
            bit = self.bit(stage)
            parts = [x.reshape(2, x.shape[0] // 2, x.shape[1]) for x in (kept, came)]

            def half(place):
                own, new = (lax.dynamic_index_in_dim(x, place, 0, keepdims=False) for x in parts)
                return own + new

            sent, kept = half(1 - bit), half(bit)
            came = self.swap(sent, stage)
        value = kept + came
        value = value + self.swap(value, last)
        for stage in range(last - 1, -1, -1):
            came = self.swap(value, stage)
            bit = self.bit(stage)
            whole = jnp.zeros((2,) + value.shape, value.dtype)
            whole = lax.dynamic_update_index_in_dim(whole, value, bit, 0)
            whole = lax.dynamic_update_index_in_dim(whole, came, 1 - bit, 0)
            value = whole.reshape(-1, value.shape[1])
        return value, self.swap(value, None)


def per_device(groups, inner, unfolding, start_basis):
    parts = gram(unfolding)
    exchange = Exchange(groups, inner)
    halves = []
    for number in range(len(CHUNKS)):
        halves += exchange.all_sum(*parts[2 * number : 2 * number + 2])
    factor, core_block = iterate(start_basis, halves, unfolding)
    return (factor, core_block)


def solution(mesh):
    in_specs = (P(None, ("grp", "in")), P())
    out_specs = (P(), P(None, ("grp", "in")))
    body = functools.partial(per_device, mesh.shape["grp"], mesh.shape["in"])
    return jax.shard_map(body, mesh=mesh, in_specs=in_specs, out_specs=out_specs, check_vma=False)
```

time: 110 us -> 103 us (0.936)
  Pallas kernels: 53.6 us -> 48.1 us
  waiting for transfers between devices: 27.2 us -> 24.7 us
  starting transfers between devices: 24.7 us -> 26.5 us
    pallas_call x2, Pallas kernels: 53.6 us -> 48.1 us  [the longest x1 29 us: iterate(): pl.pallas_call(functools.partial(iterate_kernel, bs), in_specs=[hbm] + [v...]
    ppermute x18, waiting for transfers between devices: 27.2 us -> 24.7 us  [swap(): return lax.ppermute(value, ('grp', 'in'), pairs)]
    ppermute x18, starting transfers between devices: 24.7 us -> 26.5 us  [swap(): return lax.ppermute(value, ('grp', 'in'), pairs)]
  transfers between devices with their start and end apart: 18 -> 18, of which waited for: 10 -> 13; matrix products, arithmetic and copies ran while one was open for 2% -> 2% of each run, Pallas kernels for 0% -> 0%
where the time goes in v1:
time: 103 us
  Pallas kernels  48.1 us (47%)
  starting transfers between devices  26.5 us (26%)
  waiting for transfers between devices  24.7 us (24%)
  other arithmetic  2.03 us (2%)
    pallas_call x1, Pallas kernels, iterate(): pl.pallas_call(functools.partial(iterate_kernel, bs), in_specs=[hbm] + [v...  29 us
    ppermute x18, starting transfers between devices, swap(): return lax.ppermute(value, ('grp', 'in'), pairs)  26.5 us
    ppermute x18, waiting for transfers between devices, swap(): return lax.ppermute(value, ('grp', 'in'), pairs)  24.7 us
    pallas_call x1, Pallas kernels, gram(): pl.pallas_call(functools.partial(gram_kernel, bs, widths), in_specs=[pl.B...  19.1 us
  transfers between devices with their start and end apart: 18, of which 13 were waited for; matrix products, arithmetic and copies ran while one was open for 2% of the time, Pallas kernels for 0%

profile of v1, /device:TPU:0, one launch (start us, length us, event | category | flops | bytes accessed | tf_op | source)
XLA Modules:
  0.0 102.7 jit_solution(2299116095178430581)
XLA Ops:
  0.6 19.1 %gram.1 = (f32[1152,128]{1,0:T(8,128)S(1)}, f32[1152,128]{1,0:T(8,128)S(1)}, f32[1152,128]{1,0:T(8,128)S(1)}, f32[1152,128]{1,0:T(8,128)S(1)}) custom-call(f32[1024,4096]{1,0:T(8,128)} %refs_4_.1), custom_call_target="tpu_custom_call" | custom-call | tf_op jit(solution)/shard_map/gram/pallas_call | solution.py:104
  20.3 1.7 %collective-permute-done.9 = f32[1152,128]{1,0:T(8,128)} collective-permute-done((f32[1152,128]{1,0:T(8,128)S(1)}, f32[1152,128]{1,0:T(8,128)}, u32[]{:S(2)}, u32[]{:S(2)}) %collective-permute-start.9) | collective-permute-done | bytes 589856 | tf_op jit(solution)/shard_map/ppermute | solution.py:313
  22.0 1.8 %dynamic-slice_add_fusion = (f32[1,576,128]{2,1,0:T(8,128)S(1)}, f32[576,128]{1,0:T(8,128)}) fusion(f32[2,576,128]{2,1,0:T(8,128)} %bitcast.20, s32[]{:T(128)S(6)} %select_n.72, f32[2,576,128]{2,1,0:T(8,128)S(1)} %bitcast.67, s32[]{:T(128)S(6)} %select_n.75), kind=kLoop, calls=%fused_computation.5 | loop fusion | flops 147456 | bytes 1769480 | tf_op jit(solution)/shard_map/add | solution.py:328
  23.9 2.9 %collective-permute-start.10 = (f32[576,128]{1,0:T(8,128)}, f32[576,128]{1,0:T(8,128)S(1)}, u32[]{:S(2)}, u32[]{:S(2)}) collective-permute-start(f32[576,128]{1,0:T(8,128)} %get-tuple-element.15), channel_id=1, source_target_pairs={{0,8},{1,17},{2,10},{3,19},{4,12},{5,21},{6,14},{7,23},{8,0},{9,25... | collective-permute-start | bytes 884744 | tf_op jit(solution)/shard_map/ppermute | solution.py:313
  26.9 4.8 %collective-permute-done.10 = f32[576,128]{1,0:T(8,128)S(1)} collective-permute-done((f32[576,128]{1,0:T(8,128)}, f32[576,128]{1,0:T(8,128)S(1)}, u32[]{:S(2)}, u32[]{:S(2)}) %collective-permute-start.10) | collective-permute-done | bytes 294944 | tf_op jit(solution)/shard_map/ppermute | solution.py:313
  31.7 2.1 %collective-permute-start.11 = (f32[288,128]{1,0:T(8,128)S(1)}, f32[288,128]{1,0:T(8,128)S(1)}, u32[]{:S(2)}, u32[]{:S(2)}) collective-permute-start(f32[288,128]{1,0:T(8,128)S(1)} %get-tuple-element.19), channel_id=1, source_target_pairs={{0,16},{1,9},{2,18},{3,11},{4,20},{5,13},{6,22},{7,15},{8,24},{9,1... | collective-permute-start | bytes 442376 | tf_op jit(solution)/shard_map/ppermute | solution.py:313
  33.8 1.8 %collective-permute-done.1 = f32[576,128]{1,0:T(8,128)S(1)} collective-permute-done((f32[576,128]{1,0:T(8,128)S(1)}, f32[576,128]{1,0:T(8,128)S(1)}, u32[]{:S(2)}, u32[]{:S(2)}) %collective-permute-start.1) | collective-permute-done | bytes 294944 | tf_op jit(solution)/shard_map/ppermute | solution.py:313
  35.6 2.4 %collective-permute-start.2 = (f32[288,128]{1,0:T(8,128)S(1)}, f32[288,128]{1,0:T(8,128)S(1)}, u32[]{:S(2)}, u32[]{:S(2)}) collective-permute-start(f32[288,128]{1,0:T(8,128)S(1)} %get-tuple-element.21), channel_id=1, source_target_pairs={{0,16},{1,9},{2,18},{3,11},{4,20},{5,13},{6,22},{7,15},{8,24},{9,1... | collective-permute-start | bytes 442376 | tf_op jit(solution)/shard_map/ppermute | solution.py:313
  38.1 1.6 %collective-permute-start.12 = (f32[144,128]{1,0:T(8,128)S(1)}, f32[144,128]{1,0:T(8,128)S(1)}, u32[]{:S(2)}, u32[]{:S(2)}) collective-permute-start(f32[144,128]{1,0:T(8,128)S(1)} %add_bitcast_fusion.4), channel_id=1, source_target_pairs={{0,2},{1,3},{2,0},{3,1},{4,6},{5,7},{6,4},{7,5},{8,10},{9,11},{10,... | collective-permute-start | bytes 221192 | tf_op jit(solution)/shard_map/ppermute | solution.py:313
  39.7 1.5 %collective-permute-done.2 = f32[288,128]{1,0:T(8,128)S(1)} collective-permute-done((f32[288,128]{1,0:T(8,128)S(1)}, f32[288,128]{1,0:T(8,128)S(1)}, u32[]{:S(2)}, u32[]{:S(2)}) %collective-permute-start.2) | collective-permute-done | bytes 147488 | tf_op jit(solution)/shard_map/ppermute | solution.py:313
  41.2 2.1 %collective-permute-start.3 = (f32[144,128]{1,0:T(8,128)S(1)}, f32[144,128]{1,0:T(8,128)S(1)}, u32[]{:S(2)}, u32[]{:S(2)}) collective-permute-start(f32[144,128]{1,0:T(8,128)S(1)} %add_bitcast_fusion.5), channel_id=1, source_target_pairs={{0,2},{1,3},{2,0},{3,1},{4,6},{5,7},{6,4},{7,5},{8,10},{9,11},{10,... | collective-permute-start | bytes 221192 | tf_op jit(solution)/shard_map/ppermute | solution.py:313
  43.4 2.7 %collective-permute-start.13 = (f32[144,128]{1,0:T(8,128)S(1)}, f32[144,128]{1,0:T(8,128)S(1)}, u32[]{:S(2)}, u32[]{:S(2)}) collective-permute-start(f32[144,128]{1,0:T(8,128)S(1)} %bitcast_add_fusion), channel_id=1, source_target_pairs={{0,4},{1,5},{2,6},{3,7},{4,0},{5,1},{6,2},{7,3},{8,12},{9,13},{10,... | collective-permute-start | bytes 221192 | tf_op jit(solution)/shard_map/ppermute | solution.py:313
  46.0 3.3 %collective-permute-start.4 = (f32[144,128]{1,0:T(8,128)S(1)}, f32[144,128]{1,0:T(8,128)S(1)}, u32[]{:S(2)}, u32[]{:S(2)}) collective-permute-start(f32[144,128]{1,0:T(8,128)S(1)} %bitcast_add_fusion.1), channel_id=1, source_target_pairs={{0,4},{1,5},{2,6},{3,7},{4,0},{5,1},{6,2},{7,3},{8,12},{9,13},{10,... | collective-permute-start | bytes 221192 | tf_op jit(solution)/shard_map/ppermute | solution.py:313
  51.8 1.7 %collective-permute-start.5 = (f32[144,128]{1,0:T(8,128)S(1)}, f32[144,128]{1,0:T(8,128)S(1)}, u32[]{:S(2)}, u32[]{:S(2)}) collective-permute-start(f32[144,128]{1,0:T(8,128)S(1)} %get-tuple-element.13), channel_id=1, source_target_pairs={{0,2},{1,3},{2,0},{3,1},{4,6},{5,7},{6,4},{7,5},{8,10},{9,11},{10,... | collective-permute-start | bytes 221192 | tf_op jit(solution)/shard_map/ppermute | solution.py:313
  54.6 1.6 %collective-permute-start.15 = (f32[288,128]{1,0:T(8,128)S(1)}, f32[288,128]{1,0:T(8,128)S(1)}, u32[]{:S(2)}, u32[]{:S(2)}) collective-permute-start(f32[288,128]{1,0:T(8,128)S(1)} %bitcast.77), channel_id=1, source_target_pairs={{0,16},{1,9},{2,18},{3,11},{4,20},{5,13},{6,22},{7,15},{8,24},{9,1... | collective-permute-start | bytes 442376 | tf_op jit(solution)/shard_map/ppermute | solution.py:313
  56.2 1.6 %collective-permute-start.6 = (f32[288,128]{1,0:T(8,128)S(1)}, f32[288,128]{1,0:T(8,128)S(1)}, u32[]{:S(2)}, u32[]{:S(2)}) collective-permute-start(f32[288,128]{1,0:T(8,128)S(1)} %bitcast.75), channel_id=1, source_target_pairs={{0,16},{1,9},{2,18},{3,11},{4,20},{5,13},{6,22},{7,15},{8,24},{9,1... | collective-permute-start | bytes 442376 | tf_op jit(solution)/shard_map/ppermute | solution.py:313
  57.9 3.5 %collective-permute-done.15 = f32[288,128]{1,0:T(8,128)S(1)} collective-permute-done((f32[288,128]{1,0:T(8,128)S(1)}, f32[288,128]{1,0:T(8,128)S(1)}, u32[]{:S(2)}, u32[]{:S(2)}) %collective-permute-start.15) | collective-permute-done | bytes 147488 | tf_op jit(solution)/shard_map/ppermute | solution.py:313
  61.4 1.6 %collective-permute-start.16 = (f32[576,128]{1,0:T(8,128)S(1)}, f32[576,128]{1,0:T(8,128)S(1)}, u32[]{:S(2)}, u32[]{:S(2)}) collective-permute-start(f32[576,128]{1,0:T(8,128)S(1)} %bitcast.70), channel_id=1, source_target_pairs={{0,8},{1,17},{2,10},{3,19},{4,12},{5,21},{6,14},{7,23},{8,0},{9,25... | collective-permute-start | bytes 884744 | tf_op jit(solution)/shard_map/ppermute | solution.py:313
  63.0 1.6 %collective-permute-done.6 = f32[288,128]{1,0:T(8,128)S(1)} collective-permute-done((f32[288,128]{1,0:T(8,128)S(1)}, f32[288,128]{1,0:T(8,128)S(1)}, u32[]{:S(2)}, u32[]{:S(2)}) %collective-permute-start.6) | collective-permute-done | bytes 147488 | tf_op jit(solution)/shard_map/ppermute | solution.py:313
  64.6 1.6 %collective-permute-start.7 = (f32[576,128]{1,0:T(8,128)S(1)}, f32[576,128]{1,0:T(8,128)S(1)}, u32[]{:S(2)}, u32[]{:S(2)}) collective-permute-start(f32[576,128]{1,0:T(8,128)S(1)} %bitcast.68), channel_id=1, source_target_pairs={{0,8},{1,17},{2,10},{3,19},{4,12},{5,21},{6,14},{7,23},{8,0},{9,25... | collective-permute-start | bytes 884744 | tf_op jit(solution)/shard_map/ppermute | solution.py:313
  66.3 1.9 %collective-permute-done.16 = f32[576,128]{1,0:T(8,128)S(1)} collective-permute-done((f32[576,128]{1,0:T(8,128)S(1)}, f32[576,128]{1,0:T(8,128)S(1)}, u32[]{:S(2)}, u32[]{:S(2)}) %collective-permute-start.16) | collective-permute-done | bytes 294944 | tf_op jit(solution)/shard_map/ppermute | solution.py:313
  68.3 3.1 %collective-permute-done.7 = f32[576,128]{1,0:T(8,128)S(1)} collective-permute-done((f32[576,128]{1,0:T(8,128)S(1)}, f32[576,128]{1,0:T(8,128)S(1)}, u32[]{:S(2)}, u32[]{:S(2)}) %collective-permute-start.7) | collective-permute-done | bytes 294944 | tf_op jit(solution)/shard_map/ppermute | solution.py:313
  71.5 2.0 %collective-permute-done.8.refs_1_ = f32[1152,128]{1,0:T(8,128)S(1)} collective-permute-done((f32[1152,128]{1,0:T(8,128)S(1)}, f32[1152,128]{1,0:T(8,128)S(1)}, u32[]{:S(2)}, u32[]{:S(2)}) %collective-permute-start.8) | collective-permute-done | bytes 589856 | tf_op jit(solution)/shard_map/ppermute | solution.py:313
  73.5 29.0 %iterate.1 = (f32[1024,128]{1,0:T(8,128)}, f32[128,4096]{1,0:T(8,128)}) custom-call(f32[1024,128]{1,0:T(8,128)S(1)} %copy-done, f32[1152,128]{1,0:T(8,128)S(1)} %bitcast.63, f32[1152,128]{1,0:T(8,128)S(1)} %collective-permute-done.8.refs_1_, f32[1152,128]{1,0:T(8,128)S(1)} %bitcast.65, f32[1152,128]{1,0:T(8,128)S(1)} %collective-permute-done.17.refs_3_, ...), custom_call_target="tpu_custom_call" | custom-call | tf_op jit(solution)/shard_map/iterate/pallas_call | solution.py:271
  (42 shorter events, 4.9 us)
Async XLA Ops:
  0.6 72.9 %copy-start = (f32[1024,128]{1,0:T(8,128)S(1)}, f32[1024,128]{1,0:T(8,128)}, u32[]{:S(2)}) copy-start(f32[1024,128]{1,0:T(8,128)} %start_hbm.1) | copy-start | bytes 1572868
  19.7 2.3 %collective-permute-start.9 = (f32[1152,128]{1,0:T(8,128)S(1)}, f32[1152,128]{1,0:T(8,128)}, u32[]{:S(2)}, u32[]{:S(2)}) collective-permute-start(f32[1152,128]{1,0:T(8,128)S(1)} %get-tuple-element.9), channel_id=1, source_target_pairs={{0,1},{1,0},{2,3},{3,2},{4,5},{5,4},{6,7},{7,6},{8,9},{9,8},{10,11... | collective-permute-start | bytes 1769480 | tf_op jit(solution)/shard_map/ppermute | solution.py:313
  20.2 6.5 %collective-permute-start = (f32[1152,128]{1,0:T(8,128)S(1)}, f32[1152,128]{1,0:T(8,128)S(1)}, u32[]{:S(2)}, u32[]{:S(2)}) collective-permute-start(f32[1152,128]{1,0:T(8,128)S(1)} %get-tuple-element.7), channel_id=1, source_target_pairs={{0,1},{1,0},{2,3},{3,2},{4,5},{5,4},{6,7},{7,6},{8,9},{9,8},{10,11... | collective-permute-start | bytes 1769480 | tf_op jit(solution)/shard_map/ppermute | solution.py:313
  23.9 7.8 %collective-permute-start.10 = (f32[576,128]{1,0:T(8,128)}, f32[576,128]{1,0:T(8,128)S(1)}, u32[]{:S(2)}, u32[]{:S(2)}) collective-permute-start(f32[576,128]{1,0:T(8,128)} %get-tuple-element.15), channel_id=1, source_target_pairs={{0,8},{1,17},{2,10},{3,19},{4,12},{5,21},{6,14},{7,23},{8,0},{9,25... | collective-permute-start | bytes 884744 | tf_op jit(solution)/shard_map/ppermute | solution.py:313
  26.8 8.8 %collective-permute-start.1 = (f32[576,128]{1,0:T(8,128)S(1)}, f32[576,128]{1,0:T(8,128)S(1)}, u32[]{:S(2)}, u32[]{:S(2)}) collective-permute-start(f32[576,128]{1,0:T(8,128)S(1)} %get-tuple-element.17), channel_id=1, source_target_pairs={{0,8},{1,17},{2,10},{3,19},{4,12},{5,21},{6,14},{7,23},{8,0},{9,25... | collective-permute-start | bytes 884744 | tf_op jit(solution)/shard_map/ppermute | solution.py:313
  31.7 6.4 %collective-permute-start.11 = (f32[288,128]{1,0:T(8,128)S(1)}, f32[288,128]{1,0:T(8,128)S(1)}, u32[]{:S(2)}, u32[]{:S(2)}) collective-permute-start(f32[288,128]{1,0:T(8,128)S(1)} %get-tuple-element.19), channel_id=1, source_target_pairs={{0,16},{1,9},{2,18},{3,11},{4,20},{5,13},{6,22},{7,15},{8,24},{9,1... | collective-permute-start | bytes 442376 | tf_op jit(solution)/shard_map/ppermute | solution.py:313
  35.6 5.5 %collective-permute-start.2 = (f32[288,128]{1,0:T(8,128)S(1)}, f32[288,128]{1,0:T(8,128)S(1)}, u32[]{:S(2)}, u32[]{:S(2)}) collective-permute-start(f32[288,128]{1,0:T(8,128)S(1)} %get-tuple-element.21), channel_id=1, source_target_pairs={{0,16},{1,9},{2,18},{3,11},{4,20},{5,13},{6,22},{7,15},{8,24},{9,1... | collective-permute-start | bytes 442376 | tf_op jit(solution)/shard_map/ppermute | solution.py:313
  38.1 5.3 %collective-permute-start.12 = (f32[144,128]{1,0:T(8,128)S(1)}, f32[144,128]{1,0:T(8,128)S(1)}, u32[]{:S(2)}, u32[]{:S(2)}) collective-permute-start(f32[144,128]{1,0:T(8,128)S(1)} %add_bitcast_fusion.4), channel_id=1, source_target_pairs={{0,2},{1,3},{2,0},{3,1},{4,6},{5,7},{6,4},{7,5},{8,10},{9,11},{10,... | collective-permute-start | bytes 221192 | tf_op jit(solution)/shard_map/ppermute | solution.py:313
  41.2 4.8 %collective-permute-start.3 = (f32[144,128]{1,0:T(8,128)S(1)}, f32[144,128]{1,0:T(8,128)S(1)}, u32[]{:S(2)}, u32[]{:S(2)}) collective-permute-start(f32[144,128]{1,0:T(8,128)S(1)} %add_bitcast_fusion.5), channel_id=1, source_target_pairs={{0,2},{1,3},{2,0},{3,1},{4,6},{5,7},{6,4},{7,5},{8,10},{9,11},{10,... | collective-permute-start | bytes 221192 | tf_op jit(solution)/shard_map/ppermute | solution.py:313
  43.4 6.8 %collective-permute-start.13 = (f32[144,128]{1,0:T(8,128)S(1)}, f32[144,128]{1,0:T(8,128)S(1)}, u32[]{:S(2)}, u32[]{:S(2)}) collective-permute-start(f32[144,128]{1,0:T(8,128)S(1)} %bitcast_add_fusion), channel_id=1, source_target_pairs={{0,4},{1,5},{2,6},{3,7},{4,0},{5,1},{6,2},{7,3},{8,12},{9,13},{10,... | collective-permute-start | bytes 221192 | tf_op jit(solution)/shard_map/ppermute | solution.py:313
  46.0 5.7 %collective-permute-start.4 = (f32[144,128]{1,0:T(8,128)S(1)}, f32[144,128]{1,0:T(8,128)S(1)}, u32[]{:S(2)}, u32[]{:S(2)}) collective-permute-start(f32[144,128]{1,0:T(8,128)S(1)} %bitcast_add_fusion.1), channel_id=1, source_target_pairs={{0,4},{1,5},{2,6},{3,7},{4,0},{5,1},{6,2},{7,3},{8,12},{9,13},{10,... | collective-permute-start | bytes 221192 | tf_op jit(solution)/shard_map/ppermute | solution.py:313
  50.1 4.4 %collective-permute-start.14 = (f32[144,128]{1,0:T(8,128)S(1)}, f32[144,128]{1,0:T(8,128)S(1)}, u32[]{:S(2)}, u32[]{:S(2)}) collective-permute-start(f32[144,128]{1,0:T(8,128)S(1)} %get-tuple-element.11), channel_id=1, source_target_pairs={{0,2},{1,3},{2,0},{3,1},{4,6},{5,7},{6,4},{7,5},{8,10},{9,11},{10,... | collective-permute-start | bytes 221192 | tf_op jit(solution)/shard_map/ppermute | solution.py:313
  51.8 4.4 %collective-permute-start.5 = (f32[144,128]{1,0:T(8,128)S(1)}, f32[144,128]{1,0:T(8,128)S(1)}, u32[]{:S(2)}, u32[]{:S(2)}) collective-permute-start(f32[144,128]{1,0:T(8,128)S(1)} %get-tuple-element.13), channel_id=1, source_target_pairs={{0,2},{1,3},{2,0},{3,1},{4,6},{5,7},{6,4},{7,5},{8,10},{9,11},{10,... | collective-permute-start | bytes 221192 | tf_op jit(solution)/shard_map/ppermute | solution.py:313
  54.6 6.9 %collective-permute-start.15 = (f32[288,128]{1,0:T(8,128)S(1)}, f32[288,128]{1,0:T(8,128)S(1)}, u32[]{:S(2)}, u32[]{:S(2)}) collective-permute-start(f32[288,128]{1,0:T(8,128)S(1)} %bitcast.77), channel_id=1, source_target_pairs={{0,16},{1,9},{2,18},{3,11},{4,20},{5,13},{6,22},{7,15},{8,24},{9,1... | collective-permute-start | bytes 442376 | tf_op jit(solution)/shard_map/ppermute | solution.py:313
  56.2 8.3 %collective-permute-start.6 = (f32[288,128]{1,0:T(8,128)S(1)}, f32[288,128]{1,0:T(8,128)S(1)}, u32[]{:S(2)}, u32[]{:S(2)}) collective-permute-start(f32[288,128]{1,0:T(8,128)S(1)} %bitcast.75), channel_id=1, source_target_pairs={{0,16},{1,9},{2,18},{3,11},{4,20},{5,13},{6,22},{7,15},{8,24},{9,1... | collective-permute-start | bytes 442376 | tf_op jit(solution)/shard_map/ppermute | solution.py:313
  61.4 6.8 %collective-permute-start.16 = (f32[576,128]{1,0:T(8,128)S(1)}, f32[576,128]{1,0:T(8,128)S(1)}, u32[]{:S(2)}, u32[]{:S(2)}) collective-permute-start(f32[576,128]{1,0:T(8,128)S(1)} %bitcast.70), channel_id=1, source_target_pairs={{0,8},{1,17},{2,10},{3,19},{4,12},{5,21},{6,14},{7,23},{8,0},{9,25... | collective-permute-start | bytes 884744 | tf_op jit(solution)/shard_map/ppermute | solution.py:313
  64.6 6.8 %collective-permute-start.7 = (f32[576,128]{1,0:T(8,128)S(1)}, f32[576,128]{1,0:T(8,128)S(1)}, u32[]{:S(2)}, u32[]{:S(2)}) collective-permute-start(f32[576,128]{1,0:T(8,128)S(1)} %bitcast.68), channel_id=1, source_target_pairs={{0,8},{1,17},{2,10},{3,19},{4,12},{5,21},{6,14},{7,23},{8,0},{9,25... | collective-permute-start | bytes 884744 | tf_op jit(solution)/shard_map/ppermute | solution.py:313
  68.3 3.2 %collective-permute-start.17 = (f32[1152,128]{1,0:T(8,128)S(1)}, f32[1152,128]{1,0:T(8,128)S(1)}, u32[]{:S(2)}, u32[]{:S(2)}) collective-permute-start(f32[1152,128]{1,0:T(8,128)S(1)} %bitcast.64), channel_id=1, source_target_pairs={{0,1},{1,0},{2,3},{3,2},{4,5},{5,4},{6,7},{7,6},{8,9},{9,8},{10,11... | collective-permute-start | bytes 1769480 | tf_op jit(solution)/shard_map/ppermute | solution.py:313
  71.4 2.1 %collective-permute-start.8 = (f32[1152,128]{1,0:T(8,128)S(1)}, f32[1152,128]{1,0:T(8,128)S(1)}, u32[]{:S(2)}, u32[]{:S(2)}) collective-permute-start(f32[1152,128]{1,0:T(8,128)S(1)} %bitcast.62), channel_id=1, source_target_pairs={{0,1},{1,0},{2,3},{3,2},{4,5},{5,4},{6,7},{7,6},{8,9},{9,8},{10,11... | collective-permute-start | bytes 1769480 | tf_op jit(solution)/shard_map/ppermute | solution.py:313
